TPU v7x, 768 devices: a whole 4x8x12 slice. The times are simulated.
768 devices in a mesh: rep: 192 (over z, y, core), tp: 4 (over x).
Axes of the slice: x: 4, y: 8, z: 12, core: 2. Of those that a mesh axis runs over, the one named last changes fastest.
Arguments:
- grads: bfloat16 [192, 128, 22016], P('rep', None, 'tp'), may hold values from -135 to 135
- error: bfloat16 [192, 128, 22016], P('rep', None, 'tp'), may hold values from -3 to 3
- q_prev: float32 [22016, 32], P('tp'), may hold values from -6 to 6
Outputs:
- ortho_basis: float32 [128, 32], replicated
- q_next: float32 [22016, 32], P('tp')
- error_next: bfloat16 [192, 128, 22016], P('rep', None, 'tp')
All inputs are finite; a program needn't handle non-finite values.
Results may differ from a plain program's by a relative error of at most 0.001.
Values sent between devices are 32-bit elements; how exact they have to be, the bound alone decides.
A program may use at most 32 MiB of HBM per device.

v0:
```python
import jax
import jax.numpy as jnp
from jax import lax
from jax.sharding import PartitionSpec as P


def shards(grads, error, q_prev):
    highest = lax.Precision.HIGHEST
    merged = grads[0].astype(jnp.float32) + error[0].astype(jnp.float32)
    partial_value = jnp.dot(merged, q_prev, precision=highest, preferred_element_type=jnp.float32)
    row_share = lax.psum_scatter(partial_value, "tp", scatter_dimension=0, tiled=True)
    row_total = lax.psum(row_share, "rep")
    gram_share = jnp.einsum(
        "rk,rj->kj", row_total, row_total, precision=highest, preferred_element_type=jnp.float32
    )
    gram_matrix = lax.psum(gram_share, "tp")
    cholesky_factor = jnp.linalg.cholesky(gram_matrix)
    basis_share = lax.linalg.triangular_solve(
        cholesky_factor, row_total, left_side=False, lower=True, transpose_a=True
    )
    ortho_basis = lax.all_gather(basis_share, "tp", axis=0, tiled=True)
    q_partial = jnp.einsum(
        "rc,rk->ck", merged, ortho_basis, precision=highest, preferred_element_type=jnp.float32
    )
    q_next = lax.psum(q_partial, "rep") / lax.axis_size("rep")
    approx = jnp.einsum(
        "rk,ck->rc", ortho_basis, q_next, precision=highest, preferred_element_type=jnp.float32
    )
    error_next = (merged - approx).astype(jnp.bfloat16)[None]
    return (ortho_basis, q_next, error_next)


def solution(mesh):
    in_specs = (P("rep", None, "tp"), P("rep", None, "tp"), P("tp", None))
    out_specs = (P(), P("tp", None), P("rep", None, "tp"))
    return jax.shard_map(shards, mesh=mesh, in_specs=in_specs, out_specs=out_specs, check_vma=False)
```

profile of v0, /device:TPU:1, one launch (start us, length us, event | category | flops | bytes accessed | tf_op | source)
XLA Modules:
  0.0 1128.5 jit_solution(1464881777575877663)
XLA Ops:
  7.2 0.0 copy-start
  7.2 0.0 copy-start.1
  7.2 0.0 copy-start.2
  7.2 0.0 reduce-scatter.2.cloned.1.call-start
  7.2 1.0 copy-done
  8.3 4.9 fusion.4
  13.1 0.0 reduce-scatter.2.cloned.1.call-update
  13.2 0.0 all-reduce.2.cloned.1.call-start
  13.2 34.0 %reduce-scatter.2.cloned.1.call-done = f32[32,32]{1,0:T(8,128)} async-done(((f32[128,32]{1,0:T(8,128)}), f32[32,32]{1,0:T(8,128)}) %reduce-scatter.2.cloned.1.call-update) | async-done | bytes 4112 | tf_op jit(solution)/shard_map/reduce_scatter | solution.py:11
  47.2 736.8 %psum.21 = f32[32,32]{1,0:T(8,128)S(1)} all-reduce(f32[32,32]{1,0:T(8,128)} %reduce-scatter.2.cloned.1.call-done), channel_id=1, replica_groups=mesh['rep'=192,'tp'=4] {'rep'}, use_global_device_ids=true, to_apply=%region_1.0 | all-reduce | flops 1024 | bytes 8192 | tf_op jit(solution)/shard_map/psum | solution.py:12
  784.0 0.8 fusion.10
  784.9 12.4 %psum.22 = f32[32,32]{0,1:T(8,128)S(1)} all-reduce(f32[32,32]{0,1:T(8,128)} %fusion.10), channel_id=1, replica_groups=mesh['rep'=192,'tp'=4] {'tp'}, use_global_device_ids=true, to_apply=%region_2.0 | all-reduce | flops 1024 | bytes 8192 | tf_op jit(solution)/shard_map/psum | solution.py:16
  797.3 0.7 copy.7
  798.0 1.3 fusion.9
  799.3 3.6 cholesky.16
  802.9 0.6 compare_reduce_fusion
  803.6 1.3 fusion.6
  804.8 3.2 custom-call.6
  808.0 0.2 fusion.7
  808.2 9.0 all_gather.3
  817.1 0.6 copy-done.4
  817.8 0.0 copy-done.1
  817.8 0.0 copy-done.2
  817.8 2.7 fusion.2
  820.5 0.0 all-reduce.2.cloned.1.call-update
  820.5 1.5 copy.8
  822.1 294.7 %all-reduce.2.cloned.1.call-done = f32[5504,32]{0,1:T(8,128)} async-done(((f32[5504,32]{0,1:T(8,128)}), f32[5504,32]{0,1:T(8,128)}) %all-reduce.2.cloned.1.call-update) | async-done | bytes 704528 | tf_op jit(solution)/shard_map/psum | solution.py:25
  1116.8 1.2 broadcast_multiply_fusion
  1118.0 0.0 copy-done.5
  1118.0 0.0 copy-start.3
  1118.0 3.6 fusion.1
  1121.7 0.0 copy-done.3
  (3 shorter events, 0.0 us)
Async XLA Ops:
  7.2 1.1 copy-start
  7.2 810.6 %copy-start.1 = (bf16[1,128,5504]{2,1,0:T(8,128)(2,1)S(1)}, bf16[1,128,5504]{2,1,0:T(8,128)(2,1)}, u32[]{:S(2)}) copy-start(bf16[1,128,5504]{2,1,0:T(8,128)(2,1)} %param.4) | copy-start | bytes 4227076
  7.2 810.6 %copy-start.2 = (bf16[1,128,5504]{2,1,0:T(8,128)(2,1)S(1)}, bf16[1,128,5504]{2,1,0:T(8,128)(2,1)}, u32[]{:S(2)}) copy-start(bf16[1,128,5504]{2,1,0:T(8,128)(2,1)} %param.3) | copy-start | bytes 4227076
  7.2 40.0 %reduce-scatter.2.cloned.1.call-start = ((), (), s32[]{:S(2)}) async-start(), calls=%async_computation.1 | async-start | bytes 81920 | tf_op jit(solution)/shard_map/reduce_scatter | solution.py:11
  13.2 1103.6 %all-reduce.2.cloned.1.call-start = ((), (), s32[]{:S(2)}) async-start(), calls=%async_computation.2 | async-start | bytes 1409024 | tf_op jit(solution)/shard_map/psum | solution.py:25
  817.1 0.6 copy-start.4
  1116.8 1.2 copy-start.5
  1118.0 3.6 copy-start.3
Sparse Core Ops, SparseCore 0:
  13.3 33.8 reduce-scatter.1
  820.7 296.0 all-reduce.1
where the time goes:
time: 1130 us
  blocking collectives  758 us (67%)
  waiting for transfers between devices  329 us (29%)
  between operations  14.1 us (1%)
  matrix products  12.2 us (1%)
    psum x1, blocking collectives, shards(): row_total = lax.psum(row_share, 'rep')  737 us
    psum x1, waiting for transfers between devices, shards(): q_next = lax.psum(q_partial, 'rep') / lax.axis_size('rep')  295 us
    reduce_scatter x1, waiting for transfers between devices, shards(): lax.psum_scatter(partial_value, 'tp', scatter_dimension=0, tiled=True)  34 us
  transfers between devices with their start and end apart: 2, of which 2 were waited for; matrix products, arithmetic and copies ran while one was open for 0% of the time, Pallas kernels for 0%

commit v1 on v0

v1 whole, which is shorter than its diff:
```python
import functools

import jax
import jax.numpy as jnp
from jax import lax
from jax.experimental import pallas as pl
from jax.experimental.pallas import tpu as pltpu
from jax.sharding import PartitionSpec as P

NZ, NY, NX = 12, 8, 4
ROWS, RANK = 128, 32
REPLICAS = 192
LOCAL = 5504
TILES = LOCAL // 128
ATOMS_A, ATOMS_B = 40, 48
ATOMS = ATOMS_A + ATOMS_B
REAL = 2 * TILES
CHUNKS = ((0, 11), (11, 11), (22, 11), (33, 10))
MESH = pl.DeviceIdType.MESH
F32, BF16 = jnp.float32, jnp.bfloat16


def split3(v):
    hi = v.astype(BF16)
    rest = v - hi.astype(F32)
    mid = rest.astype(BF16)
    lo = (rest - mid.astype(F32)).astype(BF16)
    return hi, mid, lo


def far_first(n):
    return sorted(range(1, n), key=lambda k: (-min(k, n - k), k))


def drain(ref, sem):
    pltpu.make_async_copy(ref, ref, sem).wait()


def dot_f32(a, b, dims):
    return lax.dot_general(a, b, (dims, ((), ())), precision=lax.Precision.HIGHEST, preferred_element_type=F32)


def inverse_factor(gram):
    row = lax.broadcasted_iota(jnp.int32, (RANK, 128), 0)
    lane = lax.broadcasted_iota(jnp.int32, (RANK, 128), 1)
    work = jnp.concatenate([gram, jnp.zeros((RANK, 128 - RANK), F32)], axis=1)
    work = work + (lane == row + RANK).astype(F32)

    def step(k, work):
        at_row = jnp.sum(jnp.where(row == k, work, 0.0), axis=0, keepdims=True)
        column = jnp.sum(jnp.where(lane == k, work, 0.0), axis=1, keepdims=True)
        pivot = jnp.sum(jnp.where(lane[:1] == k, at_row, 0.0), axis=1, keepdims=True)
        scale = 1.0 / jnp.sqrt(pivot)
        scaled = at_row * scale
        reduced = work - (column * scale) * scaled
        return jnp.where(row == k, scaled, jnp.where(row > k, reduced, work))

    return lax.fori_loop(0, RANK, step, work)[:, RANK : 2 * RANK]


def reduce_kernel(
    g_ref, e_ref, q_ref, out_ref, small,
    ge, qv, f_part, f_core, f_x, f_y, f_z, f_full,
    p_part, p_core, p_sum, a_one, b_one, a_two, b_two, fin,
    load_sem, out_sem, ssem, rsem,
):
    rep, x = lax.axis_index("rep"), lax.axis_index("tp")
    c = lax.rem(rep, 2)
    y = lax.rem(rep // 2, NY)
    z = rep // (2 * NY)

    def at(zz, yy, cc, xx):
        return {"rep": (zz * NY + yy) * 2 + cc, "tp": xx}

    def on_x(k):
        return lax.rem(x + k, NX)

    def on_y(k):
        return lax.rem(y + k, NY)

    def on_z(k):
        return lax.rem(z + k, NZ)

    other = at(z, y, 1 - c, x)
    xs = [at(z, y, c, on_x(k)) for k in far_first(NX)]
    ys = [(on_y(k), at(z, on_y(k), c, x)) for k in far_first(NY)]
    zs = [(on_z(k), at(on_z(k), y, c, x)) for k in far_first(NZ)]

    def send(src, dst, sem, device):
        pltpu.make_async_remote_copy(
            src_ref=src, dst_ref=dst, send_sem=ssem.at[sem], recv_sem=rsem.at[sem], device_id=device, device_id_type=MESH
        ).start()

    loads = []
    for i, (t0, nt) in enumerate(CHUNKS):
        cols = pl.ds(t0 * 128, nt * 128)
        group = [
            pltpu.make_async_copy(q_ref.at[:, cols], qv.at[:, cols], load_sem.at[3 * i]),
            pltpu.make_async_copy(g_ref.at[0, :, cols], ge.at[pl.ds(0, ROWS), cols], load_sem.at[3 * i + 1]),
            pltpu.make_async_copy(e_ref.at[0, :, cols], ge.at[pl.ds(ROWS, ROWS), cols], load_sem.at[3 * i + 2]),
        ]
        for copy in group:
            copy.start()
        loads.append(group)

    barrier = pltpu.get_barrier_semaphore()
    partners = [other] + xs + [d for _, d in ys] + [d for _, d in zs]
    for device in partners:
        pl.semaphore_signal(barrier, inc=1, device_id=device, device_id_type=MESH)

    both = jnp.zeros((3 * RANK, 2 * ROWS), F32)
    for (t0, nt), group in zip(CHUNKS, loads, strict=True):
        for copy in group:
            copy.wait()
        cols = pl.ds(t0 * 128, nt * 128)
        left = jnp.concatenate(split3(qv[:, cols]), axis=0)
        both += lax.dot_general(left, ge[:, cols], (((1,), (1,)), ((), ())), preferred_element_type=F32)
    both = both[:, :ROWS] + both[:, ROWS:]
    part = both[:RANK] + (both[RANK : 2 * RANK] + both[2 * RANK :])
    f_part[...] = part.reshape(4, 8, 128)
    p_part[:, pl.ds(REAL, ATOMS - REAL)] = jnp.zeros((2, ATOMS - REAL, 8, 128), F32)
    pl.semaphore_wait(barrier, len(partners))

    send(f_part.at[pl.ds(2 * (1 - c), 2)], f_core, 0, other)
    drain(f_core, rsem.at[0])
    f_x[x] = f_part[pl.ds(2 * c, 2)] + f_core[...]
    for device in xs:
        send(f_x.at[x], f_x.at[x], 1, device)
    drain(f_x.at[pl.ds(0, NX - 1)], rsem.at[1])
    f_y[y] = functools.reduce(jnp.add, [f_x[k] for k in range(NX)])
    for _, device in ys:
        send(f_y.at[y], f_y.at[y], 2, device)
    drain(f_y.at[pl.ds(0, NY - 1)], rsem.at[2])
    f_z[z] = functools.reduce(jnp.add, [f_y[k] for k in range(NY)])
    for _, device in zs:
        send(f_z.at[z], f_z.at[z], 3, device)
    drain(f_z.at[pl.ds(0, NZ - 1)], rsem.at[3])
    f_full[pl.ds(2 * c, 2)] = functools.reduce(jnp.add, [f_z[k] for k in range(NZ)])
    send(f_full.at[pl.ds(2 * c, 2)], f_full.at[pl.ds(2 * c, 2)], 4, other)
    drain(f_full.at[pl.ds(0, 2)], rsem.at[4])
    factor = f_full[...].reshape(RANK, ROWS)

    left = jnp.concatenate(split3(factor), axis=0)
    left = jnp.concatenate([left, left], axis=1)
    for i, (t0, nt) in enumerate(CHUNKS):
        three = jnp.dot(left, ge[:, pl.ds(t0 * 128, nt * 128)], preferred_element_type=F32)
        term = three[:RANK] + (three[RANK : 2 * RANK] + three[2 * RANK :])
        for t in range(nt):
            for r in range(4):
                p_part[r // 2, (r % 2) * TILES + t0 + t] = term[8 * r : 8 * r + 8, 128 * t : 128 * t + 128]
        for r in range(2):
            atoms = pl.ds(r * TILES + t0, nt)
            send(p_part.at[1 - c, atoms], p_core.at[atoms], 5 + i, other)
    p_core[pl.ds(REAL, ATOMS - REAL)] = jnp.zeros((ATOMS - REAL, 8, 128), F32)
    for i, (t0, nt) in enumerate(CHUNKS):
        drain(p_core.at[pl.ds(0, 2 * nt)], rsem.at[5 + i])
    p_sum[...] = p_part[c] + p_core[...]

    na, nb = ATOMS_A // NY, ATOMS_B // NZ
    for yy, device in ys:
        send(p_sum.at[pl.ds(na * yy, na)], a_one.at[y], 9, device)
    for zz, device in zs:
        send(p_sum.at[pl.ds(ATOMS_A + nb * zz, nb)], b_one.at[z], 10, device)
    a_one[y] = p_sum[pl.ds(na * y, na)]
    b_one[z] = p_sum[pl.ds(ATOMS_A + nb * z, nb)]

    inverse = inverse_factor(dot_f32(factor, factor, ((1,), (1,))))
    ortho = dot_f32(inverse, factor, ((1,), (0,)))
    small[0] = ortho
    small[1] = jnp.concatenate([inverse, jnp.zeros((RANK, 128 - RANK), F32)], axis=1)

    drain(a_one.at[pl.ds(0, NY - 1)], rsem.at[9])
    a_two[z] = functools.reduce(jnp.add, [a_one[k] for k in range(NY)])
    for _, device in zs:
        send(a_two.at[z], a_two.at[z], 11, device)
    drain(b_one.at[pl.ds(0, NZ - 1)], rsem.at[10])
    b_two[y] = functools.reduce(jnp.add, [b_one[k] for k in range(NZ)])
    for _, device in ys:
        send(b_two.at[y], b_two.at[y], 12, device)

    drain(b_two.at[pl.ds(0, NY - 1)], rsem.at[12])
    own = pl.ds(ATOMS_A + nb * z, nb)
    fin[c, own] = functools.reduce(jnp.add, [b_two[k] for k in range(NY)])
    for _, device in zs:
        send(fin.at[c, own], fin.at[c, own], 14, device)
    drain(a_two.at[pl.ds(0, NZ - 1)], rsem.at[11])
    own = pl.ds(na * y, na)
    fin[c, own] = functools.reduce(jnp.add, [a_two[k] for k in range(NZ)])
    for _, device in ys:
        send(fin.at[c, own], fin.at[c, own], 13, device)

    part_a, part_b = pl.ds(0, ATOMS_A), pl.ds(ATOMS_A, ATOMS_B)
    drain(fin.at[c, pl.ds(0, ATOMS_A - na)], rsem.at[13])
    send(fin.at[c, part_a], fin.at[c, part_a], 15, other)
    drain(fin.at[c, pl.ds(0, ATOMS_B - nb)], rsem.at[14])
    send(fin.at[c, part_b], fin.at[c, part_b], 16, other)
    drain(fin.at[c, part_a], rsem.at[15])
    drain(fin.at[c, part_b], rsem.at[16])
    out = pltpu.make_async_copy(fin, out_ref, out_sem.at[0])
    out.start()

    drain(f_core, ssem.at[0])
    drain(f_x.at[pl.ds(0, NX - 1)], ssem.at[1])
    drain(f_y.at[pl.ds(0, NY - 1)], ssem.at[2])
    drain(f_z.at[pl.ds(0, NZ - 1)], ssem.at[3])
    drain(f_full.at[pl.ds(0, 2)], ssem.at[4])
    for i, (_, nt) in enumerate(CHUNKS):
        drain(p_core.at[pl.ds(0, 2 * nt)], ssem.at[5 + i])
    drain(a_one.at[pl.ds(0, NY - 1)], ssem.at[9])
    drain(b_one.at[pl.ds(0, NZ - 1)], ssem.at[10])
    drain(a_two.at[pl.ds(0, NZ - 1)], ssem.at[11])
    drain(b_two.at[pl.ds(0, NY - 1)], ssem.at[12])
    drain(fin.at[c, pl.ds(0, ATOMS_A - na)], ssem.at[13])
    drain(fin.at[c, pl.ds(0, ATOMS_B - nb)], ssem.at[14])
    drain(fin.at[c, part_a], ssem.at[15])
    drain(fin.at[c, part_b], ssem.at[16])
    out.wait()


def apply_kernel(g_ref, e_ref, p_ref, small, ortho_ref, q_ref, error_ref, gv, ev, pv, qv, err, load_sem, out_sem):
    whole = pltpu.make_async_copy(p_ref, pv, load_sem.at[2 * len(CHUNKS)])
    whole.start()
    loads = []
    for i, (t0, nt) in enumerate(CHUNKS):
        cols = pl.ds(t0 * 128, nt * 128)
        group = [
            pltpu.make_async_copy(g_ref.at[0, :, cols], gv.at[:, cols], load_sem.at[2 * i]),
            pltpu.make_async_copy(e_ref.at[0, :, cols], ev.at[:, cols], load_sem.at[2 * i + 1]),
        ]
        for copy in group:
            copy.start()
        loads.append(group)
    ortho_t = small[0]
    ortho_ref[...] = ortho_t
    first = stack_left(small[1][:, :RANK])
    second = stack_left(jnp.swapaxes(ortho_t, 0, 1))
    whole.wait()
    outs = []
    for i, (t0, nt) in enumerate(CHUNKS):
        cols = pl.ds(t0 * 128, nt * 128)
        total = jnp.concatenate(
            [jnp.concatenate([pv[r // 2, (r % 2) * TILES + t0 + t] for t in range(nt)], axis=1) for r in range(4)], axis=0
        )
        q_next = jnp.dot(first, stack_right(total), preferred_element_type=F32) / REPLICAS
        qv[:, cols] = q_next
        outs.append(pltpu.make_async_copy(qv.at[:, cols], q_ref.at[:, cols], out_sem.at[2 * i]))
        outs[-1].start()
        approx = jnp.dot(second, stack_right(q_next), preferred_element_type=F32)
        for copy in loads[i]:
            copy.wait()
        merged = gv[:, cols].astype(F32) + ev[:, cols].astype(F32)
        err[:, cols] = (merged - approx).astype(BF16)
        outs.append(pltpu.make_async_copy(err.at[:, cols], error_ref.at[0, :, cols], out_sem.at[2 * i + 1]))
        outs[-1].start()
    for copy in outs:
        copy.wait()


def stack_left(v):
    hi, mid, lo = split3(v)
    return jnp.concatenate([hi, hi, hi, mid, mid, lo], axis=1)


def stack_right(v):
    hi, mid, lo = split3(v)
    return jnp.concatenate([hi, mid, lo, hi, mid, hi], axis=0)


def shards(grads, error, q_prev):
    na, nb = ATOMS_A // NY, ATOMS_B // NZ
    n_chunks = len(CHUNKS)
    vmem, anywhere = pl.BlockSpec(memory_space=pltpu.VMEM), pl.BlockSpec(memory_space=pl.ANY)

    def atoms(*lead):
        return pltpu.VMEM((*lead, 8, 128), F32)

    total, small = pl.pallas_call(
        reduce_kernel,
        out_shape=(jax.ShapeDtypeStruct((2, ATOMS, 8, 128), F32), jax.ShapeDtypeStruct((2, RANK, 128), F32)),
        in_specs=[anywhere] * 3,
        out_specs=(anywhere, vmem),
        scratch_shapes=[
            pltpu.VMEM((2 * ROWS, LOCAL), BF16),
            pltpu.VMEM((RANK, LOCAL), F32),
            atoms(4), atoms(2), atoms(NX, 2), atoms(NY, 2), atoms(NZ, 2), atoms(4),
            atoms(2, ATOMS), atoms(ATOMS), atoms(ATOMS),
            atoms(NY, na), atoms(NZ, nb), atoms(NZ, na), atoms(NY, nb), atoms(2, ATOMS),
            pltpu.SemaphoreType.DMA((3 * n_chunks,)),
            pltpu.SemaphoreType.DMA((1,)),
            pltpu.SemaphoreType.DMA((17,)),
            pltpu.SemaphoreType.DMA((17,)),
        ],
        compiler_params=pltpu.CompilerParams(collective_id=0, has_side_effects=True, vmem_limit_bytes=20 * 2**20),
        name="reduce_factors",
    )(grads, error, jnp.swapaxes(q_prev, 0, 1))
    ortho_t, q_t, error_next = pl.pallas_call(
        apply_kernel,
        out_shape=(
            jax.ShapeDtypeStruct((RANK, ROWS), F32),
            jax.ShapeDtypeStruct((RANK, LOCAL), F32),
            jax.ShapeDtypeStruct((1, ROWS, LOCAL), BF16),
        ),
        in_specs=[anywhere] * 3 + [vmem],
        out_specs=(vmem, anywhere, anywhere),
        scratch_shapes=[
            pltpu.VMEM((ROWS, LOCAL), BF16),
            pltpu.VMEM((ROWS, LOCAL), BF16),
            atoms(2, ATOMS),
            pltpu.VMEM((RANK, LOCAL), F32),
            pltpu.VMEM((ROWS, LOCAL), BF16),
            pltpu.SemaphoreType.DMA((2 * n_chunks + 1,)),
            pltpu.SemaphoreType.DMA((2 * n_chunks,)),
        ],
        compiler_params=pltpu.CompilerParams(vmem_limit_bytes=20 * 2**20),
        name="apply_factors",
    )(grads, error, total, small)
    return jnp.swapaxes(ortho_t, 0, 1), jnp.swapaxes(q_t, 0, 1), error_next


def solution(mesh):
    in_specs = (P("rep", None, "tp"), P("rep", None, "tp"), P("tp", None))
    out_specs = (P(), P("tp", None), P("rep", None, "tp"))
    return jax.shard_map(shards, mesh=mesh, in_specs=in_specs, out_specs=out_specs, check_vma=False)
```

time: 1130 us -> 73.2 us (0.06)
  blocking collectives: 758 us -> 0 us
  waiting for transfers between devices: 329 us -> 0 us
  Pallas kernels: 0 us -> 68.5 us
  between operations: 14.1 us -> 0.65 us
  matrix products: 12.2 us -> 0 us
    psum x2 -> x0, blocking collectives: 749 us -> none  [the longest x1 737 us: shards(): row_total = lax.psum(row_share, 'rep')]
    psum x1 -> x0, waiting for transfers between devices: 295 us -> none  [shards(): q_next = lax.psum(q_partial, 'rep') / lax.axis_size('rep')]
    pallas_call x0 -> x2, Pallas kernels: none -> 68.5 us  [the longest x1 64.1 us: shards(): pl.pallas_call(reduce_kernel, out_shape=(jax.ShapeDtypeStruct((2, ATOMS,...]
    reduce_scatter x1 -> x0, waiting for transfers between devices: 34 us -> none  [shards(): lax.psum_scatter(partial_value, 'tp', scatter_dimension=0, tiled=True)]
    dot_general x4 -> x0, matrix products: 12.1 us -> none  [the longest x1 4.86 us: shards(): jnp.dot(merged, q_prev, precision=highest, preferred_element_type=jnp.flo...]
  transfers between devices with their start and end apart: 2 -> 0, of which waited for: 2 -> 0; matrix products, arithmetic and copies ran while one was open for 0% -> 0% of each run, Pallas kernels for 0% -> 0%
where the time goes in v1:
time: 73.2 us; the launch traced here: 73 us
  Pallas kernels  68.5 us (94%)
  local copies, waits for them, and re-layouts  3.8 us (5%)
    pallas_call x1, Pallas kernels, shards(): pl.pallas_call(reduce_kernel, out_shape=(jax.ShapeDtypeStruct((2, ATOMS,...  64.1 us
    pallas_call x1, Pallas kernels, shards(): pl.pallas_call(apply_kernel, out_shape=(jax.ShapeDtypeStruct((RANK, ROWS)...  4.48 us
    unnamed x6, local copies, waits for them, and re-layouts  3.8 us

profile of v1, /device:TPU:1, one launch (start us, length us, event | category | flops | bytes accessed | tf_op | source)
XLA Modules:
  0.0 73.0 jit_solution(18231997343637744915)
XLA Ops:
  0.6 0.0 copy-start
  0.6 1.3 %copy-done = bf16[1,128,5504]{2,1,0:T(8,128)(2,1)S(1)} copy-done((bf16[1,128,5504]{2,1,0:T(8,128)(2,1)S(1)}, bf16[1,128,5504]{2,1,0:T(8,128)(2,1)}, u32[]{:S(2)}) %copy-start) | copy-done | bytes 1409048
  2.0 0.0 copy-start.1
  2.0 1.3 %copy-done.1 = bf16[1,128,5504]{2,1,0:T(8,128)(2,1)S(1)} copy-done((bf16[1,128,5504]{2,1,0:T(8,128)(2,1)S(1)}, bf16[1,128,5504]{2,1,0:T(8,128)(2,1)}, u32[]{:S(2)}) %copy-start.1) | copy-done | bytes 1409048
  3.3 0.0 copy-start.2
  3.3 1.1 %copy-done.2 = f32[5504,32]{0,1:T(8,128)S(1)} copy-done((f32[5504,32]{0,1:T(8,128)S(1)}, f32[5504,32]{0,1:T(8,128)}, u32[]{:S(2)}) %copy-start.2) | copy-done | bytes 704536
  4.4 64.1 %reduce_factors.1 = (f32[2,88,8,128]{3,2,1,0:T(8,128)S(1)}, f32[2,32,128]{2,1,0:T(8,128)S(1)}) custom-call(bf16[1,128,5504]{2,1,0:T(8,128)(2,1)S(1)} %copy-done, bf16[1,128,5504]{2,1,0:T(8,128)(2,1)S(1)} %copy-done.1, f32[32,5504]{1,0:T(8,128)S(1)} %bitcast.3), custom_call_target="tpu_custom_call" | custom-call | tf_op jit(solution)/shard_map/reduce_factors/pallas_call | solution.py:277
  68.5 4.5 %apply_factors.1 = (f32[32,128]{1,0:T(8,128)}, f32[32,5504]{1,0:T(8,128)}, bf16[1,128,5504]{2,1,0:T(8,128)(2,1)}) custom-call(bf16[1,128,5504]{2,1,0:T(8,128)(2,1)S(1)} %copy-done, bf16[1,128,5504]{2,1,0:T(8,128)(2,1)S(1)} %copy-done.1, f32[2,88,8,128]{3,2,1,0:T(8,128)S(1)} %get-tuple-element.8.p_ref, f32[2,32,128]{2,1,0:T(8,128)S(1)} %get-tuple-element.9.small), custom_call_target="tpu_custom_call" | custom-call | tf_op jit(solution)/shard_map/apply_factors/pallas_call | solution.py:296
Async XLA Ops:
  0.6 1.4 %copy-start = (bf16[1,128,5504]{2,1,0:T(8,128)(2,1)S(1)}, bf16[1,128,5504]{2,1,0:T(8,128)(2,1)}, u32[]{:S(2)}) copy-start(bf16[1,128,5504]{2,1,0:T(8,128)(2,1)} %g_ref.3) | copy-start | bytes 4227076
  2.0 1.4 %copy-start.1 = (bf16[1,128,5504]{2,1,0:T(8,128)(2,1)S(1)}, bf16[1,128,5504]{2,1,0:T(8,128)(2,1)}, u32[]{:S(2)}) copy-start(bf16[1,128,5504]{2,1,0:T(8,128)(2,1)} %e_ref.3) | copy-start | bytes 4227076
  3.3 1.1 %copy-start.2 = (f32[5504,32]{0,1:T(8,128)S(1)}, f32[5504,32]{0,1:T(8,128)}, u32[]{:S(2)}) copy-start(f32[5504,32]{0,1:T(8,128)} %param.5) | copy-start | bytes 2113540

commit v2 on v1

v2 whole, which is shorter than its diff:
```python
import functools

import jax
import jax.numpy as jnp
from jax import lax
from jax.experimental import pallas as pl
from jax.experimental.pallas import tpu as pltpu
from jax.sharding import PartitionSpec as P

NZ, NY, NX = 12, 8, 4
ROWS, RANK = 128, 32
REPLICAS = 192
LOCAL = 5504
TILES = LOCAL // 128
ATOMS_A, ATOMS_B = 40, 48
TILES_B = 23
ATOMS = ATOMS_A + ATOMS_B
CHUNKS = ((0, 12), (12, 11), (23, 10), (33, 10))
MESH = pl.DeviceIdType.MESH
F32, BF16 = jnp.float32, jnp.bfloat16


def split3(v):
    hi = v.astype(BF16)
    rest = v - hi.astype(F32)
    mid = rest.astype(BF16)
    lo = (rest - mid.astype(F32)).astype(BF16)
    return hi, mid, lo


def atom_of(tile):
    return 2 * tile if tile < TILES_B else ATOMS_B + 2 * (tile - TILES_B)


def far_first(n):
    return sorted(range(1, n), key=lambda k: (-min(k, n - k), k))


def drain(ref, sem):
    pltpu.make_async_copy(ref, ref, sem).wait()


def dot_f32(a, b, dims):
    return lax.dot_general(a, b, (dims, ((), ())), precision=lax.Precision.HIGHEST, preferred_element_type=F32)


def inverse_factor(gram):
    row = lax.broadcasted_iota(jnp.int32, (RANK, 128), 0)
    lane = lax.broadcasted_iota(jnp.int32, (RANK, 128), 1)
    work = jnp.concatenate([gram, jnp.zeros((RANK, 128 - RANK), F32)], axis=1)
    work = work + (lane == row + RANK).astype(F32)

    def step(k, work):
        column = jnp.sum(jnp.where(lane == k, work, 0.0), axis=1, keepdims=True)
        at_row = jnp.sum(jnp.where(row == k, work, 0.0), axis=0, keepdims=True)
        pivot = jnp.sum(jnp.where(row[:, :1] == k, column, 0.0), axis=0, keepdims=True)
        scale = lax.rsqrt(pivot)
        scale = scale * (1.5 - 0.5 * (pivot * scale) * scale)
        scaled = at_row * scale
        reduced = work - jnp.where(row[:, :1] > k, column * scale, 0.0) * scaled
        return jnp.where(row == k, scaled, reduced)

    return lax.fori_loop(0, RANK, step, work)[:, RANK : 2 * RANK]


def reduce_kernel(
    until, g_ref, e_ref, q_ref, ge, fin, small,
    qv, f_part, f_cx, f_y, f_z, f_full, p_part, p_core, p_sum, a_one, b_one, a_sum, a_two, b_two,
    load_sem, ssem, rsem,
):
    rep, x = lax.axis_index("rep"), lax.axis_index("tp")
    c = lax.rem(rep, 2)
    y = lax.rem(rep // 2, NY)
    z = rep // (2 * NY)
    na, nb = ATOMS_A // NY, ATOMS_B // NZ

    def at(zz, yy, cc, xx):
        return {"rep": (zz * NY + yy) * 2 + cc, "tp": xx}

    other = at(z, y, 1 - c, x)
    xs = [(k, lax.rem(x + k, NX)) for k in far_first(NX)]
    cxs = [(lax.rem(c + flip, 2), at(z, y, lax.rem(c + flip, 2), xx)) for flip in (1, 0) for _, xx in xs]
    cxs.append((1 - c, other))
    ys = [(yy, at(z, yy, c, x)) for yy in [lax.rem(y + k, NY) for k in far_first(NY)]]
    zs = [(zz, at(zz, y, c, x)) for zz in [lax.rem(z + k, NZ) for k in far_first(NZ)]]
    sent = []

    def send(src, dst, sem, device):
        pltpu.make_async_remote_copy(
            src_ref=src, dst_ref=dst, send_sem=ssem.at[sem], recv_sem=rsem.at[sem], device_id=device, device_id_type=MESH
        ).start()

    def arrive(ref, sem):
        drain(ref, rsem.at[sem])
        sent.append((ref, sem))

    def finish():
        for ref, sem in sent:
            drain(ref, ssem.at[sem])

    loads = []
    for i, (t0, nt) in enumerate(CHUNKS):
        cols = pl.ds(t0 * 128, nt * 128)
        group = [
            pltpu.make_async_copy(q_ref.at[:, cols], qv.at[:, cols], load_sem.at[3 * i]),
            pltpu.make_async_copy(g_ref.at[0, :, cols], ge.at[pl.ds(0, ROWS), cols], load_sem.at[3 * i + 1]),
            pltpu.make_async_copy(e_ref.at[0, :, cols], ge.at[pl.ds(ROWS, ROWS), cols], load_sem.at[3 * i + 2]),
        ]
        for copy in group:
            copy.start()
        loads.append(group)

    barrier = pltpu.get_barrier_semaphore()
    partners = [d for _, d in cxs] + [d for _, d in ys] + [d for _, d in zs]
    for device in partners:
        pl.semaphore_signal(barrier, inc=1, device_id=device, device_id_type=MESH)

    both = jnp.zeros((3 * RANK, 2 * ROWS), F32)
    for (t0, nt), group in zip(CHUNKS, loads, strict=True):
        for copy in group:
            copy.wait()
        cols = pl.ds(t0 * 128, nt * 128)
        left = jnp.concatenate(split3(qv[:, cols]), axis=0)
        both += lax.dot_general(left, ge[:, cols], (((1,), (1,)), ((), ())), preferred_element_type=F32)
    both = both[:, :ROWS] + both[:, ROWS:]
    part = both[:RANK] + (both[RANK : 2 * RANK] + both[2 * RANK :])
    f_part[...] = part.reshape(4, 8, 128)
    pad = pl.ds(2 * TILES_B, ATOMS_B - 2 * TILES_B)
    p_sum[pad] = jnp.zeros((ATOMS_B - 2 * TILES_B, 8, 128), F32)
    pl.semaphore_wait(barrier, len(partners))
    if until == 0:
        return finish()

    own = 2 * x + c
    for cc, device in cxs:
        send(f_part.at[pl.ds(2 * cc, 2)], f_cx.at[own], 0, device)
    f_cx[own] = f_part[pl.ds(2 * c, 2)]
    arrive(f_cx.at[pl.ds(0, 2 * NX - 1)], 0)
    if until == 1:
        return finish()
    f_y[y] = functools.reduce(jnp.add, [f_cx[k] for k in range(2 * NX)])
    for _, device in ys:
        send(f_y.at[y], f_y.at[y], 1, device)
    arrive(f_y.at[pl.ds(0, NY - 1)], 1)
    if until == 2:
        return finish()
    f_z[z] = functools.reduce(jnp.add, [f_y[k] for k in range(NY)])
    for _, device in zs:
        send(f_z.at[z], f_z.at[z], 2, device)
    arrive(f_z.at[pl.ds(0, NZ - 1)], 2)
    if until == 3:
        return finish()
    half = pl.ds(2 * c, 2)
    f_full[half] = functools.reduce(jnp.add, [f_z[k] for k in range(NZ)])
    send(f_full.at[half], f_full.at[half], 3, other)
    arrive(f_full.at[pl.ds(0, 2)], 3)
    factor = f_full[...].reshape(RANK, ROWS)
    if until == 4:
        return finish()

    left = jnp.concatenate(split3(factor), axis=0)
    left = jnp.concatenate([left, left], axis=1)

    def project(i):
        t0, nt = CHUNKS[i]
        three = jnp.dot(left, ge[:, pl.ds(t0 * 128, nt * 128)], preferred_element_type=F32)
        term = three[:RANK] + (three[RANK : 2 * RANK] + three[2 * RANK :])
        for t in range(nt):
            for r in range(4):
                p_part[r // 2, atom_of(t0 + t) + r % 2] = term[8 * r : 8 * r + 8, 128 * t : 128 * t + 128]
        atoms = pl.ds(atom_of(t0), 2 * nt)
        send(p_part.at[1 - c, atoms], p_core.at[atoms], 4 + i, other)

    def add_core(i):
        t0, nt = CHUNKS[i]
        atoms = pl.ds(atom_of(t0), 2 * nt)
        arrive(p_core.at[atoms], 4 + i)
        p_sum[atoms] = p_part[c, atoms] + p_core[atoms]

    project(0)
    project(1)
    project(2)
    add_core(0)
    add_core(1)
    for zz, device in zs:
        send(p_sum.at[pl.ds(nb * zz, nb)], b_one.at[z], 8, device)
    b_one[z] = p_sum[pl.ds(nb * z, nb)]
    project(3)
    add_core(2)
    add_core(3)
    for yy, device in ys:
        send(p_sum.at[pl.ds(ATOMS_B + na * yy, na)], a_one.at[y], 9, device)
    a_one[y] = p_sum[pl.ds(ATOMS_B + na * y, na)]

    if until != 6:
        inverse = inverse_factor(dot_f32(factor, factor, ((1,), (1,))))
        small[0] = dot_f32(inverse, factor, ((1,), (0,)))
        small[1] = jnp.concatenate([inverse, jnp.zeros((RANK, 128 - RANK), F32)], axis=1)
    owners = [NZ * j // na for j in range(na)]
    owned = [z == zz for zz in owners]
    is_owner = functools.reduce(jnp.logical_or, owned)
    arrive(a_one.at[pl.ds(0, NY - 1)], 9)
    if until == 5 or until == 6:
        arrive(b_one.at[pl.ds(0, NZ - 1)], 8)
        return finish()
    a_sum[...] = functools.reduce(jnp.add, [a_one[k] for k in range(NY)])
    for j, zz in enumerate(owners):

        @pl.when(z != zz)
        def _(j=j, zz=zz):
            send(a_sum.at[j], a_two.at[z], 10, at(zz, y, c, x))

        @pl.when(z == zz)
        def _(j=j):
            a_two[z] = a_sum[j]

    arrive(b_one.at[pl.ds(0, NZ - 1)], 8)
    b_two[y] = functools.reduce(jnp.add, [b_one[k] for k in range(NZ)])
    for _, device in ys:
        send(b_two.at[y], b_two.at[y], 11, device)

    for j in range(na):

        @pl.when(owned[j])
        def _(j=j):
            drain(a_two.at[pl.ds(0, NZ - 1)], rsem.at[10])
            mine = ATOMS_B + na * y + j
            fin[c, mine] = functools.reduce(jnp.add, [a_two[k] for k in range(NZ)])
            for _, device in zs:
                send(fin.at[c, mine], fin.at[c, mine], 12, device)

    arrive(b_two.at[pl.ds(0, NY - 1)], 11)
    own_b = pl.ds(nb * z, nb)
    fin[c, own_b] = functools.reduce(jnp.add, [b_two[k] for k in range(NY)])
    for _, device in zs:
        send(fin.at[c, own_b], fin.at[c, own_b], 13, device)

    @pl.when(is_owner)
    def _():
        drain(a_sum.at[pl.ds(0, na - 1)], rsem.at[12])

    @pl.when(jnp.logical_not(is_owner))
    def _():
        drain(a_sum, rsem.at[12])

    own_a = pl.ds(ATOMS_B + na * y, na)
    for _, device in ys:
        send(fin.at[c, own_a], fin.at[c, own_a], 14, device)

    part_a, part_b = pl.ds(ATOMS_B, ATOMS_A), pl.ds(0, ATOMS_B)
    arrive(fin.at[c, pl.ds(0, ATOMS_A - na)], 14)
    send(fin.at[c, part_a], fin.at[c, part_a], 15, other)
    arrive(fin.at[c, pl.ds(0, ATOMS_B - nb)], 13)
    send(fin.at[c, part_b], fin.at[c, part_b], 16, other)
    arrive(fin.at[c, part_a], 15)
    arrive(fin.at[c, part_b], 16)

    @pl.when(is_owner)
    def _():
        drain(a_sum.at[pl.ds(0, na - 1)], ssem.at[10])
        drain(a_two.at[pl.ds(0, NZ - 1)], ssem.at[12])

    @pl.when(jnp.logical_not(is_owner))
    def _():
        drain(a_sum, ssem.at[10])

    finish()


def apply_kernel(ge, total, small, ortho_ref, q_ref, error_ref, qv, err, out_sem):
    ortho_t = small[0]
    ortho_ref[...] = ortho_t
    first = stack_left(small[1][:, :RANK])
    second = stack_left(jnp.swapaxes(ortho_t, 0, 1))
    outs = []
    for i, (t0, nt) in enumerate(CHUNKS):
        cols = pl.ds(t0 * 128, nt * 128)
        rows = [jnp.concatenate([total[r // 2, atom_of(t0 + t) + r % 2] for t in range(nt)], axis=1) for r in range(4)]
        q_next = jnp.dot(first, stack_right(jnp.concatenate(rows, axis=0)), preferred_element_type=F32) / REPLICAS
        qv[:, cols] = q_next
        outs.append(pltpu.make_async_copy(qv.at[:, cols], q_ref.at[:, cols], out_sem.at[2 * i]))
        outs[-1].start()
        approx = jnp.dot(second, stack_right(q_next), preferred_element_type=F32)
        merged = ge[pl.ds(0, ROWS), cols].astype(F32) + ge[pl.ds(ROWS, ROWS), cols].astype(F32)
        err[:, cols] = (merged - approx).astype(BF16)
        outs.append(pltpu.make_async_copy(err.at[:, cols], error_ref.at[0, :, cols], out_sem.at[2 * i + 1]))
        outs[-1].start()
    for copy in outs:
        copy.wait()


def stack_left(v):
    hi, mid, lo = split3(v)
    return jnp.concatenate([hi, hi, hi, mid, mid, lo], axis=1)


def stack_right(v):
    hi, mid, lo = split3(v)
    return jnp.concatenate([hi, mid, lo, hi, mid, hi], axis=0)


def atoms(*lead):
    return pltpu.VMEM((*lead, 8, 128), F32)


VMEM, HBM = pl.BlockSpec(memory_space=pltpu.VMEM), pl.BlockSpec(memory_space=pltpu.HBM)


def reduce_all(grads, error, q_t, until=None, collective_id=0, name="reduce_factors"):
    na, nb = ATOMS_A // NY, ATOMS_B // NZ
    return pl.pallas_call(
        functools.partial(reduce_kernel, until),
        out_shape=(
            jax.ShapeDtypeStruct((2 * ROWS, LOCAL), BF16),
            jax.ShapeDtypeStruct((2, ATOMS, 8, 128), F32),
            jax.ShapeDtypeStruct((2, RANK, 128), F32),
        ),
        in_specs=[HBM] * 3,
        out_specs=(VMEM, VMEM, VMEM),
        scratch_shapes=[
            pltpu.VMEM((RANK, LOCAL), F32),
            atoms(4), atoms(2 * NX, 2), atoms(NY, 2), atoms(NZ, 2), atoms(4),
            atoms(2, ATOMS), atoms(ATOMS), atoms(ATOMS),
            atoms(NY, na), atoms(NZ, nb), atoms(na), atoms(NZ), atoms(NY, nb),
            pltpu.SemaphoreType.DMA((3 * len(CHUNKS),)),
            pltpu.SemaphoreType.DMA((17,)),
            pltpu.SemaphoreType.DMA((17,)),
        ],
        compiler_params=pltpu.CompilerParams(collective_id=collective_id, has_side_effects=True, vmem_limit_bytes=20 * 2**20),
        name=name,
    )(*[pltpu.with_memory_space_constraint(v, pltpu.HBM) for v in (grads, error, q_t)])


def apply_all(ge, total, small):
    return pl.pallas_call(
        apply_kernel,
        out_shape=(
            jax.ShapeDtypeStruct((RANK, ROWS), F32),
            jax.ShapeDtypeStruct((RANK, LOCAL), F32),
            jax.ShapeDtypeStruct((1, ROWS, LOCAL), BF16),
        ),
        in_specs=[VMEM] * 3,
        out_specs=(VMEM, HBM, HBM),
        scratch_shapes=[
            pltpu.VMEM((RANK, LOCAL), F32),
            pltpu.VMEM((ROWS, LOCAL), BF16),
            pltpu.SemaphoreType.DMA((2 * len(CHUNKS),)),
        ],
        compiler_params=pltpu.CompilerParams(vmem_limit_bytes=20 * 2**20),
        name="apply_factors",
    )(ge, total, small)


def shards(grads, error, q_prev):
    ortho_t, q_t, error_next = apply_all(*reduce_all(grads, error, jnp.swapaxes(q_prev, 0, 1)))
    return jnp.swapaxes(ortho_t, 0, 1), jnp.swapaxes(q_t, 0, 1), error_next


def solution(mesh):
    in_specs = (P("rep", None, "tp"), P("rep", None, "tp"), P("tp", None))
    out_specs = (P(), P("tp", None), P("rep", None, "tp"))
    return jax.shard_map(shards, mesh=mesh, in_specs=in_specs, out_specs=out_specs, check_vma=False)
```

time: 73.2 us -> 67.3 us (0.919)
  local copies, waits for them, and re-layouts: 3.8 us -> 0 us
  Pallas kernels: 68.5 us -> 66.5 us
    unnamed x6 -> x0, local copies, waits for them, and re-layouts: 3.8 us -> none
    pallas_call x2, Pallas kernels: 68.5 us -> 66.5 us  [the longest x1 63.8 us: reduce_all(): pl.pallas_call(functools.partial(reduce_kernel, until), out_shape=(jax.Sh...]
where the time goes in v2:
time: 67.3 us; the launch traced here: 67.2 us
  Pallas kernels  66.5 us (99%)
    pallas_call x1, Pallas kernels, reduce_all(): pl.pallas_call(functools.partial(reduce_kernel, until), out_shape=(jax.Sh...  63.8 us
    pallas_call x1, Pallas kernels, apply_all(): pl.pallas_call(apply_kernel, out_shape=(jax.ShapeDtypeStruct((RANK, ROWS)...  2.7 us

profile of v2, /device:TPU:1, one launch (start us, length us, event | category | flops | bytes accessed | tf_op | source)
XLA Modules:
  0.0 67.2 jit_solution(6017968576208078441)
XLA Ops:
  0.6 63.8 %reduce_factors.1 = (bf16[256,5504]{1,0:T(8,128)(2,1)S(1)}, f32[2,88,8,128]{3,2,1,0:T(8,128)S(1)}, f32[2,32,128]{2,1,0:T(8,128)S(1)}) custom-call(bf16[1,128,5504]{2,1,0:T(8,128)(2,1)} %g_ref.1, bf16[1,128,5504]{2,1,0:T(8,128)(2,1)} %e_ref.1, f32[32,5504]{1,0:T(8,128)} %bitcast.3), custom_call_target="tpu_custom_call" | custom-call | tf_op jit(solution)/shard_map/reduce_factors/pallas_call | solution.py:311
  64.5 2.7 %apply_factors.1 = (f32[32,128]{1,0:T(8,128)}, f32[32,5504]{1,0:T(8,128)}, bf16[1,128,5504]{2,1,0:T(8,128)(2,1)}) custom-call(bf16[256,5504]{1,0:T(8,128)(2,1)S(1)} %get-tuple-element.9.ge, f32[2,88,8,128]{3,2,1,0:T(8,128)S(1)} %get-tuple-element.10.total, f32[2,32,128]{2,1,0:T(8,128)S(1)} %get-tuple-element.11.small), custom_call_target="tpu_custom_call" | custom-call | tf_op jit(solution)/shard_map/apply_factors/pallas_call | solution.py:335

commit v3 on v2

--- a/solution.py
+++ b/solution.py
@@ -65,7 +65,7 @@
 
 def reduce_kernel(
     until, g_ref, e_ref, q_ref, ge, fin, small,
-    qv, f_part, f_cx, f_y, f_z, f_full, p_part, p_core, p_sum, a_one, b_one, a_sum, a_two, b_two,
+    qv, f_part, f_cx, f_y, f_z, f_full, m_own, m_other, pair, p_sum, a_one, b_one, a_sum, a_two, b_two,
     load_sem, ssem, rsem,
 ):
     rep, x = lax.axis_index("rep"), lax.axis_index("tp")
@@ -135,6 +135,10 @@
     for cc, device in cxs:
         send(f_part.at[pl.ds(2 * cc, 2)], f_cx.at[own], 0, device)
     f_cx[own] = f_part[pl.ds(2 * c, 2)]
+    for i, (t0, nt) in enumerate(CHUNKS):
+        cols = pl.ds(t0 * 128, nt * 128)
+        m_own[:, cols] = ge[pl.ds(0, ROWS), cols].astype(F32) + ge[pl.ds(ROWS, ROWS), cols].astype(F32)
+        send(m_own.at[:, cols], m_other.at[:, cols], 4 + i, other)
     arrive(f_cx.at[pl.ds(0, 2 * NX - 1)], 0)
     if until == 1:
         return finish()
@@ -147,51 +151,45 @@
     f_z[z] = functools.reduce(jnp.add, [f_y[k] for k in range(NY)])
     for _, device in zs:
         send(f_z.at[z], f_z.at[z], 2, device)
+    for i, (t0, nt) in enumerate(CHUNKS):
+        cols = pl.ds(t0 * 128, nt * 128)
+        arrive(m_other.at[:, cols], 4 + i)
+        for k, piece in enumerate(split3(m_own[:, cols] + m_other[:, cols])):
+            pair[pl.ds(ROWS * k, ROWS), cols] = piece
     arrive(f_z.at[pl.ds(0, NZ - 1)], 2)
     if until == 3:
         return finish()
     half = pl.ds(2 * c, 2)
     f_full[half] = functools.reduce(jnp.add, [f_z[k] for k in range(NZ)])
     send(f_full.at[half], f_full.at[half], 3, other)
-    arrive(f_full.at[pl.ds(0, 2)], 3)
-    factor = f_full[...].reshape(RANK, ROWS)
     if until == 4:
-        return finish()
-
-    left = jnp.concatenate(split3(factor), axis=0)
-    left = jnp.concatenate([left, left], axis=1)
+        arrive(f_full.at[pl.ds(0, 2)], 3)
+        return finish()
+
+    left = jnp.concatenate(split3(f_full[half].reshape(RANK // 2, ROWS)), axis=0)
+    left = jnp.concatenate([left, left, left], axis=1)
 
     def project(i):
         t0, nt = CHUNKS[i]
-        three = jnp.dot(left, ge[:, pl.ds(t0 * 128, nt * 128)], preferred_element_type=F32)
-        term = three[:RANK] + (three[RANK : 2 * RANK] + three[2 * RANK :])
+        three = jnp.dot(left, pair[:, pl.ds(t0 * 128, nt * 128)], preferred_element_type=F32)
+        term = three[:16] + (three[16:32] + three[32:])
         for t in range(nt):
-            for r in range(4):
-                p_part[r // 2, atom_of(t0 + t) + r % 2] = term[8 * r : 8 * r + 8, 128 * t : 128 * t + 128]
-        atoms = pl.ds(atom_of(t0), 2 * nt)
-        send(p_part.at[1 - c, atoms], p_core.at[atoms], 4 + i, other)
-
-    def add_core(i):
-        t0, nt = CHUNKS[i]
-        atoms = pl.ds(atom_of(t0), 2 * nt)
-        arrive(p_core.at[atoms], 4 + i)
-        p_sum[atoms] = p_part[c, atoms] + p_core[atoms]
+            for r in range(2):
+                p_sum[atom_of(t0 + t) + r] = term[8 * r : 8 * r + 8, 128 * t : 128 * t + 128]
 
     project(0)
     project(1)
-    project(2)
-    add_core(0)
-    add_core(1)
     for zz, device in zs:
         send(p_sum.at[pl.ds(nb * zz, nb)], b_one.at[z], 8, device)
     b_one[z] = p_sum[pl.ds(nb * z, nb)]
+    project(2)
     project(3)
-    add_core(2)
-    add_core(3)
     for yy, device in ys:
         send(p_sum.at[pl.ds(ATOMS_B + na * yy, na)], a_one.at[y], 9, device)
     a_one[y] = p_sum[pl.ds(ATOMS_B + na * y, na)]
 
+    arrive(f_full.at[pl.ds(0, 2)], 3)
+    factor = f_full[...].reshape(RANK, ROWS)
     if until != 6:
         inverse = inverse_factor(dot_f32(factor, factor, ((1,), (1,))))
         small[0] = dot_f32(inverse, factor, ((1,), (0,)))
@@ -320,13 +318,13 @@
         scratch_shapes=[
             pltpu.VMEM((RANK, LOCAL), F32),
             atoms(4), atoms(2 * NX, 2), atoms(NY, 2), atoms(NZ, 2), atoms(4),
-            atoms(2, ATOMS), atoms(ATOMS), atoms(ATOMS),
+            pltpu.VMEM((ROWS, LOCAL), F32), pltpu.VMEM((ROWS, LOCAL), F32), pltpu.VMEM((3 * ROWS, LOCAL), BF16), atoms(ATOMS),
             atoms(NY, na), atoms(NZ, nb), atoms(na), atoms(NZ), atoms(NY, nb),
             pltpu.SemaphoreType.DMA((3 * len(CHUNKS),)),
             pltpu.SemaphoreType.DMA((17,)),
             pltpu.SemaphoreType.DMA((17,)),
         ],
-        compiler_params=pltpu.CompilerParams(collective_id=collective_id, has_side_effects=True, vmem_limit_bytes=20 * 2**20),
+        compiler_params=pltpu.CompilerParams(collective_id=collective_id, has_side_effects=True, vmem_limit_bytes=32 * 2**20),
         name=name,
     )(*[pltpu.with_memory_space_constraint(v, pltpu.HBM) for v in (grads, error, q_t)])
 

time: 67.3 us -> 64 us (0.951)
  Pallas kernels: 66.5 us -> 63.2 us
    pallas_call x1, Pallas kernels: 63.8 us -> 60.5 us  [reduce_all(): pl.pallas_call(functools.partial(reduce_kernel, until), out_shape=(jax.Sh...]
where the time goes in v3:
time: 64 us; the launch traced here: 63.9 us
  Pallas kernels  63.2 us (99%)
  between operations  0.64 us (1%)
    pallas_call x1, Pallas kernels, reduce_all(): pl.pallas_call(functools.partial(reduce_kernel, until), out_shape=(jax.Sh...  60.5 us
    pallas_call x1, Pallas kernels, apply_all(): pl.pallas_call(apply_kernel, out_shape=(jax.ShapeDtypeStruct((RANK, ROWS)...  2.7 us

profile of v3, /device:TPU:1, one launch (start us, length us, event | category | flops | bytes accessed | tf_op | source)
XLA Modules:
  0.0 63.9 jit_solution(17649782558103365453)
XLA Ops:
  0.6 60.5 %reduce_factors.1 = (bf16[256,5504]{1,0:T(8,128)(2,1)S(1)}, f32[2,88,8,128]{3,2,1,0:T(8,128)S(1)}, f32[2,32,128]{2,1,0:T(8,128)S(1)}) custom-call(bf16[1,128,5504]{2,1,0:T(8,128)(2,1)} %g_ref.1, bf16[1,128,5504]{2,1,0:T(8,128)(2,1)} %e_ref.1, f32[32,5504]{1,0:T(8,128)} %bitcast.3), custom_call_target="tpu_custom_call" | custom-call | tf_op jit(solution)/shard_map/reduce_factors/pallas_call | solution.py:309
  61.2 2.7 %apply_factors.1 = (f32[32,128]{1,0:T(8,128)}, f32[32,5504]{1,0:T(8,128)}, bf16[1,128,5504]{2,1,0:T(8,128)(2,1)}) custom-call(bf16[256,5504]{1,0:T(8,128)(2,1)S(1)} %get-tuple-element.9.ge, f32[2,88,8,128]{3,2,1,0:T(8,128)S(1)} %get-tuple-element.10.total, f32[2,32,128]{2,1,0:T(8,128)S(1)} %get-tuple-element.11.small), custom_call_target="tpu_custom_call" | custom-call | tf_op jit(solution)/shard_map/apply_factors/pallas_call | solution.py:333

commit v4 on v3

--- a/solution.py
+++ b/solution.py
@@ -16,6 +16,8 @@
 TILES_B = 23
 ATOMS = ATOMS_A + ATOMS_B
 CHUNKS = ((0, 12), (12, 11), (23, 10), (33, 10))
+PARTS = ((0, 23), (23, 20))
+FIRST_STEPS = 20
 MESH = pl.DeviceIdType.MESH
 F32, BF16 = jnp.float32, jnp.bfloat16
 
@@ -44,11 +46,16 @@
     return lax.dot_general(a, b, (dims, ((), ())), precision=lax.Precision.HIGHEST, preferred_element_type=F32)
 
 
-def inverse_factor(gram):
+def start_elimination(gram):
     row = lax.broadcasted_iota(jnp.int32, (RANK, 128), 0)
     lane = lax.broadcasted_iota(jnp.int32, (RANK, 128), 1)
     work = jnp.concatenate([gram, jnp.zeros((RANK, 128 - RANK), F32)], axis=1)
-    work = work + (lane == row + RANK).astype(F32)
+    return work + (lane == row + RANK).astype(F32)
+
+
+def eliminate(work, begin, end):
+    row = lax.broadcasted_iota(jnp.int32, (RANK, 128), 0)
+    lane = lax.broadcasted_iota(jnp.int32, (RANK, 128), 1)
 
     def step(k, work):
         column = jnp.sum(jnp.where(lane == k, work, 0.0), axis=1, keepdims=True)
@@ -60,12 +67,12 @@
         reduced = work - jnp.where(row[:, :1] > k, column * scale, 0.0) * scaled
         return jnp.where(row == k, scaled, reduced)
 
-    return lax.fori_loop(0, RANK, step, work)[:, RANK : 2 * RANK]
+    return lax.fori_loop(begin, end, step, work)
 
 
 def reduce_kernel(
-    until, g_ref, e_ref, q_ref, ge, fin, small,
-    qv, f_part, f_cx, f_y, f_z, f_full, m_own, m_other, pair, p_sum, a_one, b_one, a_sum, a_two, b_two,
+    until, g_ref, e_ref, q_ref, ge, fin, ortho_ref, left_ref,
+    qv, work, f_part, f_cx, f_y, f_z, f_full, m_own, m_other, pair, p_sum, a_one, b_one, a_sum, a_two, b_two,
     load_sem, ssem, rsem,
 ):
     rep, x = lax.axis_index("rep"), lax.axis_index("tp")
@@ -98,8 +105,13 @@
         for ref, sem in sent:
             drain(ref, ssem.at[sem])
 
+    barrier = pltpu.get_barrier_semaphore()
+    partners = [d for _, d in zs] + [d for _, d in ys] + [d for _, d in cxs]
+    for device in partners:
+        pl.semaphore_signal(barrier, inc=1, device_id=device, device_id_type=MESH)
+
     loads = []
-    for i, (t0, nt) in enumerate(CHUNKS):
+    for i, (t0, nt) in enumerate(PARTS):
         cols = pl.ds(t0 * 128, nt * 128)
         group = [
             pltpu.make_async_copy(q_ref.at[:, cols], qv.at[:, cols], load_sem.at[3 * i]),
@@ -110,13 +122,8 @@
             copy.start()
         loads.append(group)
 
-    barrier = pltpu.get_barrier_semaphore()
-    partners = [d for _, d in cxs] + [d for _, d in ys] + [d for _, d in zs]
-    for device in partners:
-        pl.semaphore_signal(barrier, inc=1, device_id=device, device_id_type=MESH)
-
     both = jnp.zeros((3 * RANK, 2 * ROWS), F32)
-    for (t0, nt), group in zip(CHUNKS, loads, strict=True):
+    for (t0, nt), group in zip(PARTS, loads, strict=True):
         for copy in group:
             copy.wait()
         cols = pl.ds(t0 * 128, nt * 128)
@@ -135,16 +142,18 @@
     for cc, device in cxs:
         send(f_part.at[pl.ds(2 * cc, 2)], f_cx.at[own], 0, device)
     f_cx[own] = f_part[pl.ds(2 * c, 2)]
-    for i, (t0, nt) in enumerate(CHUNKS):
+    for t0, nt in CHUNKS:
         cols = pl.ds(t0 * 128, nt * 128)
         m_own[:, cols] = ge[pl.ds(0, ROWS), cols].astype(F32) + ge[pl.ds(ROWS, ROWS), cols].astype(F32)
-        send(m_own.at[:, cols], m_other.at[:, cols], 4 + i, other)
     arrive(f_cx.at[pl.ds(0, 2 * NX - 1)], 0)
     if until == 1:
         return finish()
     f_y[y] = functools.reduce(jnp.add, [f_cx[k] for k in range(2 * NX)])
     for _, device in ys:
         send(f_y.at[y], f_y.at[y], 1, device)
+    for i, (t0, nt) in enumerate(CHUNKS):
+        cols = pl.ds(t0 * 128, nt * 128)
+        send(m_own.at[:, cols], m_other.at[:, cols], 4 + i, other)
     arrive(f_y.at[pl.ds(0, NY - 1)], 1)
     if until == 2:
         return finish()
@@ -170,7 +179,7 @@
     left = jnp.concatenate([left, left, left], axis=1)
 
     def project(i):
-        t0, nt = CHUNKS[i]
+        t0, nt = PARTS[i]
         three = jnp.dot(left, pair[:, pl.ds(t0 * 128, nt * 128)], preferred_element_type=F32)
         term = three[:16] + (three[16:32] + three[32:])
         for t in range(nt):
@@ -178,22 +187,17 @@
                 p_sum[atom_of(t0 + t) + r] = term[8 * r : 8 * r + 8, 128 * t : 128 * t + 128]
 
     project(0)
-    project(1)
     for zz, device in zs:
         send(p_sum.at[pl.ds(nb * zz, nb)], b_one.at[z], 8, device)
     b_one[z] = p_sum[pl.ds(nb * z, nb)]
-    project(2)
-    project(3)
+    project(1)
     for yy, device in ys:
         send(p_sum.at[pl.ds(ATOMS_B + na * yy, na)], a_one.at[y], 9, device)
     a_one[y] = p_sum[pl.ds(ATOMS_B + na * y, na)]
 
     arrive(f_full.at[pl.ds(0, 2)], 3)
     factor = f_full[...].reshape(RANK, ROWS)
-    if until != 6:
-        inverse = inverse_factor(dot_f32(factor, factor, ((1,), (1,))))
-        small[0] = dot_f32(inverse, factor, ((1,), (0,)))
-        small[1] = jnp.concatenate([inverse, jnp.zeros((RANK, 128 - RANK), F32)], axis=1)
+    work[...] = eliminate(start_elimination(dot_f32(factor, factor, ((1,), (1,)))), 0, FIRST_STEPS)
     owners = [NZ * j // na for j in range(na)]
     owned = [z == zz for zz in owners]
     is_owner = functools.reduce(jnp.logical_or, owned)
@@ -245,6 +249,13 @@
     for _, device in ys:
         send(fin.at[c, own_a], fin.at[c, own_a], 14, device)
 
+    inverse = eliminate(work[...], FIRST_STEPS, RANK)[:, RANK : 2 * RANK]
+    ortho_t = dot_f32(inverse, factor, ((1,), (0,)))
+    ortho_ref[...] = ortho_t
+    weights = jnp.concatenate([inverse, dot_f32(jnp.swapaxes(ortho_t, 0, 1), inverse, ((1,), (0,)))], axis=0)
+    hi, mid, lo = split3(weights * (1.0 / REPLICAS))
+    left_ref[...] = jnp.concatenate([hi, hi, hi, mid, mid, lo], axis=1)
+
     part_a, part_b = pl.ds(ATOMS_B, ATOMS_A), pl.ds(0, ATOMS_B)
     arrive(fin.at[c, pl.ds(0, ATOMS_A - na)], 14)
     send(fin.at[c, part_a], fin.at[c, part_a], 15, other)
@@ -265,31 +276,25 @@
     finish()
 
 
-def apply_kernel(ge, total, small, ortho_ref, q_ref, error_ref, qv, err, out_sem):
-    ortho_t = small[0]
-    ortho_ref[...] = ortho_t
-    first = stack_left(small[1][:, :RANK])
-    second = stack_left(jnp.swapaxes(ortho_t, 0, 1))
+def apply_kernel(ge, total, ortho, left, ortho_ref, q_ref, error_ref, qv, err, out_sem):
+    ortho_ref[...] = ortho[...]
     outs = []
     for i, (t0, nt) in enumerate(CHUNKS):
         cols = pl.ds(t0 * 128, nt * 128)
         rows = [jnp.concatenate([total[r // 2, atom_of(t0 + t) + r % 2] for t in range(nt)], axis=1) for r in range(4)]
-        q_next = jnp.dot(first, stack_right(jnp.concatenate(rows, axis=0)), preferred_element_type=F32) / REPLICAS
-        qv[:, cols] = q_next
-        outs.append(pltpu.make_async_copy(qv.at[:, cols], q_ref.at[:, cols], out_sem.at[2 * i]))
-        outs[-1].start()
-        approx = jnp.dot(second, stack_right(q_next), preferred_element_type=F32)
+        both = jnp.dot(left[...], stack_right(jnp.concatenate(rows, axis=0)), preferred_element_type=F32)
+        qv[:, cols] = both[:RANK]
         merged = ge[pl.ds(0, ROWS), cols].astype(F32) + ge[pl.ds(ROWS, ROWS), cols].astype(F32)
-        err[:, cols] = (merged - approx).astype(BF16)
-        outs.append(pltpu.make_async_copy(err.at[:, cols], error_ref.at[0, :, cols], out_sem.at[2 * i + 1]))
-        outs[-1].start()
+        err[:, cols] = (merged - both[RANK:]).astype(BF16)
+        group = [
+            pltpu.make_async_copy(qv.at[:, cols], q_ref.at[:, cols], out_sem.at[2 * i]),
+            pltpu.make_async_copy(err.at[:, cols], error_ref.at[0, :, cols], out_sem.at[2 * i + 1]),
+        ]
+        for copy in group:
+            copy.start()
+        outs += group
     for copy in outs:
         copy.wait()
-
-
-def stack_left(v):
-    hi, mid, lo = split3(v)
-    return jnp.concatenate([hi, hi, hi, mid, mid, lo], axis=1)
 
 
 def stack_right(v):
@@ -311,16 +316,18 @@
         out_shape=(
             jax.ShapeDtypeStruct((2 * ROWS, LOCAL), BF16),
             jax.ShapeDtypeStruct((2, ATOMS, 8, 128), F32),
-            jax.ShapeDtypeStruct((2, RANK, 128), F32),
+            jax.ShapeDtypeStruct((RANK, ROWS), F32),
+            jax.ShapeDtypeStruct((RANK + ROWS, 6 * RANK), BF16),
         ),
         in_specs=[HBM] * 3,
-        out_specs=(VMEM, VMEM, VMEM),
+        out_specs=(VMEM,) * 4,
         scratch_shapes=[
             pltpu.VMEM((RANK, LOCAL), F32),
+            pltpu.VMEM((RANK, 128), F32),
             atoms(4), atoms(2 * NX, 2), atoms(NY, 2), atoms(NZ, 2), atoms(4),
             pltpu.VMEM((ROWS, LOCAL), F32), pltpu.VMEM((ROWS, LOCAL), F32), pltpu.VMEM((3 * ROWS, LOCAL), BF16), atoms(ATOMS),
             atoms(NY, na), atoms(NZ, nb), atoms(na), atoms(NZ), atoms(NY, nb),
-            pltpu.SemaphoreType.DMA((3 * len(CHUNKS),)),
+            pltpu.SemaphoreType.DMA((3 * len(PARTS),)),
             pltpu.SemaphoreType.DMA((17,)),
             pltpu.SemaphoreType.DMA((17,)),
         ],
@@ -329,7 +336,7 @@
     )(*[pltpu.with_memory_space_constraint(v, pltpu.HBM) for v in (grads, error, q_t)])
 
 
-def apply_all(ge, total, small):
+def apply_all(ge, total, ortho_t, left):
     return pl.pallas_call(
         apply_kernel,
         out_shape=(
@@ -337,7 +344,7 @@
             jax.ShapeDtypeStruct((RANK, LOCAL), F32),
             jax.ShapeDtypeStruct((1, ROWS, LOCAL), BF16),
         ),
-        in_specs=[VMEM] * 3,
+        in_specs=[VMEM] * 4,
         out_specs=(VMEM, HBM, HBM),
         scratch_shapes=[
             pltpu.VMEM((RANK, LOCAL), F32),
@@ -346,7 +353,7 @@
         ],
         compiler_params=pltpu.CompilerParams(vmem_limit_bytes=20 * 2**20),
         name="apply_factors",
-    )(ge, total, small)
+    )(ge, total, ortho_t, left)
 
 
 def shards(grads, error, q_prev):

time: 64 us -> 63.3 us (0.989)
  Pallas kernels: 63.2 us -> 62.5 us
where the time goes in v4:
time: 63.3 us; the launch traced here: 63.1 us
  Pallas kernels  62.5 us (99%)
  between operations  0.64 us (1%)
    pallas_call x1, Pallas kernels, reduce_all(): pl.pallas_call(functools.partial(reduce_kernel, until), out_shape=(jax.Sh...  60.2 us
    pallas_call x1, Pallas kernels, apply_all(): pl.pallas_call(apply_kernel, out_shape=(jax.ShapeDtypeStruct((RANK, ROWS)...  2.25 us

profile of v4, /device:TPU:1, one launch (start us, length us, event | category | flops | bytes accessed | tf_op | source)
XLA Modules:
  0.0 63.1 jit_solution(9013479290980813422)
XLA Ops:
  0.6 60.2 %reduce_factors.1 = (bf16[256,5504]{1,0:T(8,128)(2,1)S(1)}, f32[2,88,8,128]{3,2,1,0:T(8,128)S(1)}, f32[32,128]{1,0:T(8,128)S(1)}, bf16[160,192]{1,0:T(8,128)(2,1)S(1)}) custom-call(bf16[1,128,5504]{2,1,0:T(8,128)(2,1)} %g_ref.1, bf16[1,128,5504]{2,1,0:T(8,128)(2,1)} %e_ref.1, f32[32,5504]{1,0:T(8,128)} %bitcast.3), custom_call_target="tpu_custom_call" | custom-call | tf_op jit(solution)/shard_map/reduce_factors/pallas_call | solution.py:314
  60.9 2.2 %apply_factors.1 = (f32[32,128]{1,0:T(8,128)}, f32[32,5504]{1,0:T(8,128)}, bf16[1,128,5504]{2,1,0:T(8,128)(2,1)}) custom-call(bf16[256,5504]{1,0:T(8,128)(2,1)S(1)} %get-tuple-element.10.ge, f32[2,88,8,128]{3,2,1,0:T(8,128)S(1)} %get-tuple-element.11.total, f32[32,128]{1,0:T(8,128)S(1)} %get-tuple-element.12.ortho, bf16[160,192]{1,0:T(8,128)(2,1)S(1)} %get-tuple-element.13.left), custom_call_target="tpu_custom_call" | custom-call | tf_op jit(solution)/shard_map/apply_factors/pallas_call | solution.py:340

commit v5 on v4

--- a/solution.py
+++ b/solution.py
@@ -186,14 +186,14 @@
             for r in range(2):
                 p_sum[atom_of(t0 + t) + r] = term[8 * r : 8 * r + 8, 128 * t : 128 * t + 128]
 
+    project(1)
+    for yy, device in ys:
+        send(p_sum.at[pl.ds(ATOMS_B + na * yy, na)], a_one.at[y], 9, device)
+    a_one[y] = p_sum[pl.ds(ATOMS_B + na * y, na)]
     project(0)
     for zz, device in zs:
         send(p_sum.at[pl.ds(nb * zz, nb)], b_one.at[z], 8, device)
     b_one[z] = p_sum[pl.ds(nb * z, nb)]
-    project(1)
-    for yy, device in ys:
-        send(p_sum.at[pl.ds(ATOMS_B + na * yy, na)], a_one.at[y], 9, device)
-    a_one[y] = p_sum[pl.ds(ATOMS_B + na * y, na)]
 
     arrive(f_full.at[pl.ds(0, 2)], 3)
     factor = f_full[...].reshape(RANK, ROWS)

time: 63.3 us -> 62.4 us (0.986)
  Pallas kernels: 62.5 us -> 61.6 us
    pallas_call x1, Pallas kernels: 60.2 us -> 59.3 us  [reduce_all(): pl.pallas_call(functools.partial(reduce_kernel, until), out_shape=(jax.Sh...]
where the time goes in v5:
time: 62.4 us; the launch traced here: 62.2 us
  Pallas kernels  61.6 us (99%)
  between operations  0.64 us (1%)
    pallas_call x1, Pallas kernels, reduce_all(): pl.pallas_call(functools.partial(reduce_kernel, until), out_shape=(jax.Sh...  59.3 us
    pallas_call x1, Pallas kernels, apply_all(): pl.pallas_call(apply_kernel, out_shape=(jax.ShapeDtypeStruct((RANK, ROWS)...  2.25 us

profile of v5, /device:TPU:1, one launch (start us, length us, event | category | flops | bytes accessed | tf_op | source)
XLA Modules:
  0.0 62.2 jit_solution(10757056667318056430)
XLA Ops:
  0.6 59.3 %reduce_factors.1 = (bf16[256,5504]{1,0:T(8,128)(2,1)S(1)}, f32[2,88,8,128]{3,2,1,0:T(8,128)S(1)}, f32[32,128]{1,0:T(8,128)S(1)}, bf16[160,192]{1,0:T(8,128)(2,1)S(1)}) custom-call(bf16[1,128,5504]{2,1,0:T(8,128)(2,1)} %g_ref.1, bf16[1,128,5504]{2,1,0:T(8,128)(2,1)} %e_ref.1, f32[32,5504]{1,0:T(8,128)} %bitcast.3), custom_call_target="tpu_custom_call" | custom-call | tf_op jit(solution)/shard_map/reduce_factors/pallas_call | solution.py:314
  60.0 2.2 %apply_factors.1 = (f32[32,128]{1,0:T(8,128)}, f32[32,5504]{1,0:T(8,128)}, bf16[1,128,5504]{2,1,0:T(8,128)(2,1)}) custom-call(bf16[256,5504]{1,0:T(8,128)(2,1)S(1)} %get-tuple-element.10.ge, f32[2,88,8,128]{3,2,1,0:T(8,128)S(1)} %get-tuple-element.11.total, f32[32,128]{1,0:T(8,128)S(1)} %get-tuple-element.12.ortho, bf16[160,192]{1,0:T(8,128)(2,1)S(1)} %get-tuple-element.13.left), custom_call_target="tpu_custom_call" | custom-call | tf_op jit(solution)/shard_map/apply_factors/pallas_call | solution.py:340

commit v6 on v5

--- a/solution.py
+++ b/solution.py
@@ -71,8 +71,8 @@
 
 
 def reduce_kernel(
-    until, g_ref, e_ref, q_ref, ge, fin, ortho_ref, left_ref,
-    qv, work, f_part, f_cx, f_y, f_z, f_full, m_own, m_other, pair, p_sum, a_one, b_one, a_sum, a_two, b_two,
+    g_ref, e_ref, q_ref, ge, fin, ortho_ref, left_ref,
+    qv, work, f_part, f_cx, f_y, f_z, f_full, m_own, m_other, pair, p_sum, a_one, b_one, a_two, b_two,
     load_sem, ssem, rsem,
 ):
     rep, x = lax.axis_index("rep"), lax.axis_index("tp")
@@ -102,7 +102,8 @@
         sent.append((ref, sem))
 
     def finish():
-        for ref, sem in sent:
+        while sent:
+            ref, sem = sent.pop(0)
             drain(ref, ssem.at[sem])
 
     barrier = pltpu.get_barrier_semaphore()
@@ -135,8 +136,6 @@
     pad = pl.ds(2 * TILES_B, ATOMS_B - 2 * TILES_B)
     p_sum[pad] = jnp.zeros((ATOMS_B - 2 * TILES_B, 8, 128), F32)
     pl.semaphore_wait(barrier, len(partners))
-    if until == 0:
-        return finish()
 
     own = 2 * x + c
     for cc, device in cxs:
@@ -146,8 +145,6 @@
         cols = pl.ds(t0 * 128, nt * 128)
         m_own[:, cols] = ge[pl.ds(0, ROWS), cols].astype(F32) + ge[pl.ds(ROWS, ROWS), cols].astype(F32)
     arrive(f_cx.at[pl.ds(0, 2 * NX - 1)], 0)
-    if until == 1:
-        return finish()
     f_y[y] = functools.reduce(jnp.add, [f_cx[k] for k in range(2 * NX)])
     for _, device in ys:
         send(f_y.at[y], f_y.at[y], 1, device)
@@ -155,8 +152,6 @@
         cols = pl.ds(t0 * 128, nt * 128)
         send(m_own.at[:, cols], m_other.at[:, cols], 4 + i, other)
     arrive(f_y.at[pl.ds(0, NY - 1)], 1)
-    if until == 2:
-        return finish()
     f_z[z] = functools.reduce(jnp.add, [f_y[k] for k in range(NY)])
     for _, device in zs:
         send(f_z.at[z], f_z.at[z], 2, device)
@@ -166,14 +161,9 @@
         for k, piece in enumerate(split3(m_own[:, cols] + m_other[:, cols])):
             pair[pl.ds(ROWS * k, ROWS), cols] = piece
     arrive(f_z.at[pl.ds(0, NZ - 1)], 2)
-    if until == 3:
-        return finish()
     half = pl.ds(2 * c, 2)
     f_full[half] = functools.reduce(jnp.add, [f_z[k] for k in range(NZ)])
     send(f_full.at[half], f_full.at[half], 3, other)
-    if until == 4:
-        arrive(f_full.at[pl.ds(0, 2)], 3)
-        return finish()
 
     left = jnp.concatenate(split3(f_full[half].reshape(RANK // 2, ROWS)), axis=0)
     left = jnp.concatenate([left, left, left], axis=1)
@@ -198,54 +188,23 @@
     arrive(f_full.at[pl.ds(0, 2)], 3)
     factor = f_full[...].reshape(RANK, ROWS)
     work[...] = eliminate(start_elimination(dot_f32(factor, factor, ((1,), (1,)))), 0, FIRST_STEPS)
-    owners = [NZ * j // na for j in range(na)]
-    owned = [z == zz for zz in owners]
-    is_owner = functools.reduce(jnp.logical_or, owned)
     arrive(a_one.at[pl.ds(0, NY - 1)], 9)
-    if until == 5 or until == 6:
-        arrive(b_one.at[pl.ds(0, NZ - 1)], 8)
-        return finish()
-    a_sum[...] = functools.reduce(jnp.add, [a_one[k] for k in range(NY)])
-    for j, zz in enumerate(owners):
-
-        @pl.when(z != zz)
-        def _(j=j, zz=zz):
-            send(a_sum.at[j], a_two.at[z], 10, at(zz, y, c, x))
-
-        @pl.when(z == zz)
-        def _(j=j):
-            a_two[z] = a_sum[j]
-
+    a_two[z] = functools.reduce(jnp.add, [a_one[k] for k in range(NY)])
+    for _, device in zs:
+        send(a_two.at[z], a_two.at[z], 10, device)
     arrive(b_one.at[pl.ds(0, NZ - 1)], 8)
     b_two[y] = functools.reduce(jnp.add, [b_one[k] for k in range(NZ)])
     for _, device in ys:
         send(b_two.at[y], b_two.at[y], 11, device)
-
-    for j in range(na):
-
-        @pl.when(owned[j])
-        def _(j=j):
-            drain(a_two.at[pl.ds(0, NZ - 1)], rsem.at[10])
-            mine = ATOMS_B + na * y + j
-            fin[c, mine] = functools.reduce(jnp.add, [a_two[k] for k in range(NZ)])
-            for _, device in zs:
-                send(fin.at[c, mine], fin.at[c, mine], 12, device)
 
     arrive(b_two.at[pl.ds(0, NY - 1)], 11)
     own_b = pl.ds(nb * z, nb)
     fin[c, own_b] = functools.reduce(jnp.add, [b_two[k] for k in range(NY)])
     for _, device in zs:
         send(fin.at[c, own_b], fin.at[c, own_b], 13, device)
-
-    @pl.when(is_owner)
-    def _():
-        drain(a_sum.at[pl.ds(0, na - 1)], rsem.at[12])
-
-    @pl.when(jnp.logical_not(is_owner))
-    def _():
-        drain(a_sum, rsem.at[12])
-
+    arrive(a_two.at[pl.ds(0, NZ - 1)], 10)
     own_a = pl.ds(ATOMS_B + na * y, na)
+    fin[c, own_a] = functools.reduce(jnp.add, [a_two[k] for k in range(NZ)])
     for _, device in ys:
         send(fin.at[c, own_a], fin.at[c, own_a], 14, device)
 
@@ -256,6 +215,7 @@
     hi, mid, lo = split3(weights * (1.0 / REPLICAS))
     left_ref[...] = jnp.concatenate([hi, hi, hi, mid, mid, lo], axis=1)
 
+    finish()
     part_a, part_b = pl.ds(ATOMS_B, ATOMS_A), pl.ds(0, ATOMS_B)
     arrive(fin.at[c, pl.ds(0, ATOMS_A - na)], 14)
     send(fin.at[c, part_a], fin.at[c, part_a], 15, other)
@@ -263,16 +223,6 @@
     send(fin.at[c, part_b], fin.at[c, part_b], 16, other)
     arrive(fin.at[c, part_a], 15)
     arrive(fin.at[c, part_b], 16)
-
-    @pl.when(is_owner)
-    def _():
-        drain(a_sum.at[pl.ds(0, na - 1)], ssem.at[10])
-        drain(a_two.at[pl.ds(0, NZ - 1)], ssem.at[12])
-
-    @pl.when(jnp.logical_not(is_owner))
-    def _():
-        drain(a_sum, ssem.at[10])
-
     finish()
 
 
@@ -309,10 +259,10 @@
 VMEM, HBM = pl.BlockSpec(memory_space=pltpu.VMEM), pl.BlockSpec(memory_space=pltpu.HBM)
 
 
-def reduce_all(grads, error, q_t, until=None, collective_id=0, name="reduce_factors"):
+def reduce_all(grads, error, q_t):
     na, nb = ATOMS_A // NY, ATOMS_B // NZ
     return pl.pallas_call(
-        functools.partial(reduce_kernel, until),
+        reduce_kernel,
         out_shape=(
             jax.ShapeDtypeStruct((2 * ROWS, LOCAL), BF16),
             jax.ShapeDtypeStruct((2, ATOMS, 8, 128), F32),
@@ -326,13 +276,13 @@
             pltpu.VMEM((RANK, 128), F32),
             atoms(4), atoms(2 * NX, 2), atoms(NY, 2), atoms(NZ, 2), atoms(4),
             pltpu.VMEM((ROWS, LOCAL), F32), pltpu.VMEM((ROWS, LOCAL), F32), pltpu.VMEM((3 * ROWS, LOCAL), BF16), atoms(ATOMS),
-            atoms(NY, na), atoms(NZ, nb), atoms(na), atoms(NZ), atoms(NY, nb),
+            atoms(NY, na), atoms(NZ, nb), atoms(NZ, na), atoms(NY, nb),
             pltpu.SemaphoreType.DMA((3 * len(PARTS),)),
             pltpu.SemaphoreType.DMA((17,)),
             pltpu.SemaphoreType.DMA((17,)),
         ],
-        compiler_params=pltpu.CompilerParams(collective_id=collective_id, has_side_effects=True, vmem_limit_bytes=32 * 2**20),
-        name=name,
+        compiler_params=pltpu.CompilerParams(collective_id=0, has_side_effects=True, vmem_limit_bytes=32 * 2**20),
+        name="reduce_factors",
     )(*[pltpu.with_memory_space_constraint(v, pltpu.HBM) for v in (grads, error, q_t)])
 
 

time: 62.4 us -> 63.6 us (1.019)
  Pallas kernels: 61.6 us -> 62.8 us
    pallas_call x1, Pallas kernels: 59.3 us -> 60.6 us  [reduce_all(): pl.pallas_call(reduce_kernel, out_shape=(jax.ShapeDtypeStruct((2 * ROWS,...]
where the time goes in v6:
time: 63.6 us; the launch traced here: 63.5 us
  Pallas kernels  62.8 us (99%)
  between operations  0.64 us (1%)
    pallas_call x1, Pallas kernels, reduce_all(): pl.pallas_call(reduce_kernel, out_shape=(jax.ShapeDtypeStruct((2 * ROWS,...  60.6 us
    pallas_call x1, Pallas kernels, apply_all(): pl.pallas_call(apply_kernel, out_shape=(jax.ShapeDtypeStruct((RANK, ROWS)...  2.25 us

profile of v6, /device:TPU:1, one launch (start us, length us, event | category | flops | bytes accessed | tf_op | source)
XLA Modules:
  0.0 63.5 jit_solution(15620489076654869931)
XLA Ops:
  0.6 60.6 %reduce_factors.1 = (bf16[256,5504]{1,0:T(8,128)(2,1)S(1)}, f32[2,88,8,128]{3,2,1,0:T(8,128)S(1)}, f32[32,128]{1,0:T(8,128)S(1)}, bf16[160,192]{1,0:T(8,128)(2,1)S(1)}) custom-call(bf16[1,128,5504]{2,1,0:T(8,128)(2,1)} %g_ref.1, bf16[1,128,5504]{2,1,0:T(8,128)(2,1)} %e_ref.1, f32[32,5504]{1,0:T(8,128)} %bitcast.3), custom_call_target="tpu_custom_call" | custom-call | tf_op jit(solution)/shard_map/reduce_factors/pallas_call | solution.py:264
  61.2 2.2 %apply_factors.1 = (f32[32,128]{1,0:T(8,128)}, f32[32,5504]{1,0:T(8,128)}, bf16[1,128,5504]{2,1,0:T(8,128)(2,1)}) custom-call(bf16[256,5504]{1,0:T(8,128)(2,1)S(1)} %get-tuple-element.10.ge, f32[2,88,8,128]{3,2,1,0:T(8,128)S(1)} %get-tuple-element.11.total, f32[32,128]{1,0:T(8,128)S(1)} %get-tuple-element.12.ortho, bf16[160,192]{1,0:T(8,128)(2,1)S(1)} %get-tuple-element.13.left), custom_call_target="tpu_custom_call" | custom-call | tf_op jit(solution)/shard_map/apply_factors/pallas_call | solution.py:290

commit v7 on v5

--- a/solution.py
+++ b/solution.py
@@ -71,7 +71,7 @@
 
 
 def reduce_kernel(
-    until, g_ref, e_ref, q_ref, ge, fin, ortho_ref, left_ref,
+    g_ref, e_ref, q_ref, ge, fin, ortho_ref, left_ref,
     qv, work, f_part, f_cx, f_y, f_z, f_full, m_own, m_other, pair, p_sum, a_one, b_one, a_sum, a_two, b_two,
     load_sem, ssem, rsem,
 ):
@@ -102,7 +102,8 @@
         sent.append((ref, sem))
 
     def finish():
-        for ref, sem in sent:
+        while sent:
+            ref, sem = sent.pop(0)
             drain(ref, ssem.at[sem])
 
     barrier = pltpu.get_barrier_semaphore()
@@ -135,8 +136,6 @@
     pad = pl.ds(2 * TILES_B, ATOMS_B - 2 * TILES_B)
     p_sum[pad] = jnp.zeros((ATOMS_B - 2 * TILES_B, 8, 128), F32)
     pl.semaphore_wait(barrier, len(partners))
-    if until == 0:
-        return finish()
 
     own = 2 * x + c
     for cc, device in cxs:
@@ -146,8 +145,6 @@
         cols = pl.ds(t0 * 128, nt * 128)
         m_own[:, cols] = ge[pl.ds(0, ROWS), cols].astype(F32) + ge[pl.ds(ROWS, ROWS), cols].astype(F32)
     arrive(f_cx.at[pl.ds(0, 2 * NX - 1)], 0)
-    if until == 1:
-        return finish()
     f_y[y] = functools.reduce(jnp.add, [f_cx[k] for k in range(2 * NX)])
     for _, device in ys:
         send(f_y.at[y], f_y.at[y], 1, device)
@@ -155,8 +152,6 @@
         cols = pl.ds(t0 * 128, nt * 128)
         send(m_own.at[:, cols], m_other.at[:, cols], 4 + i, other)
     arrive(f_y.at[pl.ds(0, NY - 1)], 1)
-    if until == 2:
-        return finish()
     f_z[z] = functools.reduce(jnp.add, [f_y[k] for k in range(NY)])
     for _, device in zs:
         send(f_z.at[z], f_z.at[z], 2, device)
@@ -166,14 +161,9 @@
         for k, piece in enumerate(split3(m_own[:, cols] + m_other[:, cols])):
             pair[pl.ds(ROWS * k, ROWS), cols] = piece
     arrive(f_z.at[pl.ds(0, NZ - 1)], 2)
-    if until == 3:
-        return finish()
     half = pl.ds(2 * c, 2)
     f_full[half] = functools.reduce(jnp.add, [f_z[k] for k in range(NZ)])
     send(f_full.at[half], f_full.at[half], 3, other)
-    if until == 4:
-        arrive(f_full.at[pl.ds(0, 2)], 3)
-        return finish()
 
     left = jnp.concatenate(split3(f_full[half].reshape(RANK // 2, ROWS)), axis=0)
     left = jnp.concatenate([left, left, left], axis=1)
@@ -202,9 +192,6 @@
     owned = [z == zz for zz in owners]
     is_owner = functools.reduce(jnp.logical_or, owned)
     arrive(a_one.at[pl.ds(0, NY - 1)], 9)
-    if until == 5 or until == 6:
-        arrive(b_one.at[pl.ds(0, NZ - 1)], 8)
-        return finish()
     a_sum[...] = functools.reduce(jnp.add, [a_one[k] for k in range(NY)])
     for j, zz in enumerate(owners):
 
@@ -256,14 +243,6 @@
     hi, mid, lo = split3(weights * (1.0 / REPLICAS))
     left_ref[...] = jnp.concatenate([hi, hi, hi, mid, mid, lo], axis=1)
 
-    part_a, part_b = pl.ds(ATOMS_B, ATOMS_A), pl.ds(0, ATOMS_B)
-    arrive(fin.at[c, pl.ds(0, ATOMS_A - na)], 14)
-    send(fin.at[c, part_a], fin.at[c, part_a], 15, other)
-    arrive(fin.at[c, pl.ds(0, ATOMS_B - nb)], 13)
-    send(fin.at[c, part_b], fin.at[c, part_b], 16, other)
-    arrive(fin.at[c, part_a], 15)
-    arrive(fin.at[c, part_b], 16)
-
     @pl.when(is_owner)
     def _():
         drain(a_sum.at[pl.ds(0, na - 1)], ssem.at[10])
@@ -273,6 +252,14 @@
     def _():
         drain(a_sum, ssem.at[10])
 
+    finish()
+    part_a, part_b = pl.ds(ATOMS_B, ATOMS_A), pl.ds(0, ATOMS_B)
+    arrive(fin.at[c, pl.ds(0, ATOMS_B - nb)], 13)
+    send(fin.at[c, part_b], fin.at[c, part_b], 16, other)
+    arrive(fin.at[c, pl.ds(0, ATOMS_A - na)], 14)
+    send(fin.at[c, part_a], fin.at[c, part_a], 15, other)
+    arrive(fin.at[c, part_b], 16)
+    arrive(fin.at[c, part_a], 15)
     finish()
 
 
@@ -309,10 +296,10 @@
 VMEM, HBM = pl.BlockSpec(memory_space=pltpu.VMEM), pl.BlockSpec(memory_space=pltpu.HBM)
 
 
-def reduce_all(grads, error, q_t, until=None, collective_id=0, name="reduce_factors"):
+def reduce_all(grads, error, q_t):
     na, nb = ATOMS_A // NY, ATOMS_B // NZ
     return pl.pallas_call(
-        functools.partial(reduce_kernel, until),
+        reduce_kernel,
         out_shape=(
             jax.ShapeDtypeStruct((2 * ROWS, LOCAL), BF16),
             jax.ShapeDtypeStruct((2, ATOMS, 8, 128), F32),
@@ -331,8 +318,8 @@
             pltpu.SemaphoreType.DMA((17,)),
             pltpu.SemaphoreType.DMA((17,)),
         ],
-        compiler_params=pltpu.CompilerParams(collective_id=collective_id, has_side_effects=True, vmem_limit_bytes=32 * 2**20),
-        name=name,
+        compiler_params=pltpu.CompilerParams(collective_id=0, has_side_effects=True, vmem_limit_bytes=32 * 2**20),
+        name="reduce_factors",
     )(*[pltpu.with_memory_space_constraint(v, pltpu.HBM) for v in (grads, error, q_t)])
 
 

time: 62.4 us -> 62.1 us (level)
  no operation moved by 1% of the time
where the time goes in v7:
time: 62.1 us; the launch traced here: 61.9 us
  Pallas kernels  61.3 us (99%)
  between operations  0.64 us (1%)
    pallas_call x1, Pallas kernels, reduce_all(): pl.pallas_call(reduce_kernel, out_shape=(jax.ShapeDtypeStruct((2 * ROWS,...  59 us
    pallas_call x1, Pallas kernels, apply_all(): pl.pallas_call(apply_kernel, out_shape=(jax.ShapeDtypeStruct((RANK, ROWS)...  2.25 us

profile of v7, /device:TPU:1, one launch (start us, length us, event | category | flops | bytes accessed | tf_op | source)
XLA Modules:
  0.0 61.9 jit_solution(16919679824474147634)
XLA Ops:
  0.6 59.0 %reduce_factors.1 = (bf16[256,5504]{1,0:T(8,128)(2,1)S(1)}, f32[2,88,8,128]{3,2,1,0:T(8,128)S(1)}, f32[32,128]{1,0:T(8,128)S(1)}, bf16[160,192]{1,0:T(8,128)(2,1)S(1)}) custom-call(bf16[1,128,5504]{2,1,0:T(8,128)(2,1)} %g_ref.1, bf16[1,128,5504]{2,1,0:T(8,128)(2,1)} %e_ref.1, f32[32,5504]{1,0:T(8,128)} %bitcast.3), custom_call_target="tpu_custom_call" | custom-call | tf_op jit(solution)/shard_map/reduce_factors/pallas_call | solution.py:301
  59.7 2.2 %apply_factors.1 = (f32[32,128]{1,0:T(8,128)}, f32[32,5504]{1,0:T(8,128)}, bf16[1,128,5504]{2,1,0:T(8,128)(2,1)}) custom-call(bf16[256,5504]{1,0:T(8,128)(2,1)S(1)} %get-tuple-element.10.ge, f32[2,88,8,128]{3,2,1,0:T(8,128)S(1)} %get-tuple-element.11.total, f32[32,128]{1,0:T(8,128)S(1)} %get-tuple-element.12.ortho, bf16[160,192]{1,0:T(8,128)(2,1)S(1)} %get-tuple-element.13.left), custom_call_target="tpu_custom_call" | custom-call | tf_op jit(solution)/shard_map/apply_factors/pallas_call | solution.py:327
